TPU v7x, 128 devices: a whole 4x4x4 slice. The times are simulated.
128 devices in a mesh: row: 4 (over z), col: 32 (over x, y, core).
Axes of the slice: x: 4, y: 4, z: 4, core: 2. Of those that a mesh axis runs over, the one named last changes fastest.
Arguments:
- evecs: float32 [1024, 65536], P('col', 'row'), may hold values from -6 to 6
- v_first: float32 [256, 65536], P('col', 'row'), may hold values from -0.046875 to 0.046875
- v_second: float32 [256, 65536], P('col', 'row'), may hold values from -0.046875 to 0.046875
- t_first: float32 [256, 256], replicated, may hold values from -0.5 to 2, as said below
- t_second: float32 [256, 256], replicated, may hold values from -0.5 to 2, as said below
Outputs:
- basis: float32 [1024, 65536], P('col', 'row')
Inputs may be any that keep to these rules, and one draw needn't show every extreme that they name: `t_first`: upper triangular, with diagonal entries between 0.5 and 2. `t_second`: upper triangular, with diagonal entries between 0.5 and 2.
All inputs are finite; a program needn't handle non-finite values.
Results may differ from a plain program's by a relative error of at most 0.00016.
Values sent between devices are 32-bit elements; how exact they have to be, the bound alone decides.
A program may use at most 128 MiB of HBM per device.

v0:
```python
import jax
import jax.numpy as jnp
from jax import lax
from jax.sharding import PartitionSpec as P


def dot_high(left, right):
    return jnp.dot(left, right, precision=lax.Precision.HIGHEST, preferred_element_type=jnp.float32)


def inner_last(left, right):
    return lax.dot_general(
        left,
        right,
        (((1,), (1,)), ((), ())),
        precision=lax.Precision.HIGHEST,
        preferred_element_type=jnp.float32,
    )


def inner_first(left, right):
    return lax.dot_general(
        left,
        right,
        (((0,), (0,)), ((), ())),
        precision=lax.Precision.HIGHEST,
        preferred_element_type=jnp.float32,
    )


def shards(evecs, v_first, v_second, t_first, t_second):
    v_one, v_two = (
        lax.all_gather(v_first, "col", axis=0, tiled=True),
        lax.all_gather(v_second, "col", axis=0, tiled=True),
    )
    matrix = evecs
    for vectors, factor in ((v_two, t_second), (v_one, t_first)):
        local_term = inner_last(vectors, matrix)
        summed = lax.psum(local_term, "row")
        matrix = matrix - inner_first(dot_high(factor, summed), vectors)
    return matrix


def solution(mesh):
    placed = (P("col", "row"), P("col", "row"), P("col", "row"), P(), P())
    return jax.shard_map(
        shards, mesh=mesh, in_specs=placed, out_specs=P("col", "row"), check_vma=False
    )
```

profile of v0, /device:TPU:0, one launch (start us, length us, event | category | flops | bytes accessed | tf_op | source)
XLA Modules:
  0.0 214.3 jit_solution(10148425127331488675)
XLA Ops:
  6.5 0.0 copy-start
  6.5 0.0 all-gather.3.cloned.1.call-start
  6.5 0.7 all-gather.3.cloned.1.call-update
  7.3 0.0 all-gather.5.cloned.1.call-start
  7.3 0.7 all-gather.5.cloned.1.call-update
  8.0 76.5 %all-gather.3.cloned.1.call-done = f32[256,16384]{1,0:T(8,128)} async-done(((f32[8,16384]{1,0:T(8,128)}), f32[256,16384]{1,0:T(8,128)}) %all-gather.3.cloned.1.call-update) | async-done | bytes 16777232 | tf_op jit(solution)/shard_map/all_gather | solution.py:34
  84.5 15.9 %fusion = f32[256,32]{1,0:T(8,128)S(1)} fusion(f32[256,16384]{1,0:T(8,128)} %all-gather.3.cloned.1.call-done, f32[32,16384]{1,0:T(8,128)} %param.5), kind=kOutput, calls=%fused_computation.3 | convolution fusion | flops 1610612736 | bytes 18907136 | tf_op jit(solution)/shard_map/dot_general | solution.py:12
  100.4 18.9 %psum.14 = f32[256,32]{1,0:T(8,128)S(1)} all-reduce(f32[256,32]{1,0:T(8,128)S(1)} %fusion), channel_id=1, replica_groups=mesh['row'=4,'col'=32] {'row'}, use_global_device_ids=true, to_apply=%region_0.0 | all-reduce | flops 8192 | bytes 65536 | tf_op jit(solution)/shard_map/psum | solution.py:39
  119.3 0.0 copy-done
  119.3 0.3 fusion.1
  119.7 13.9 %convolution_subtract_fusion.1 = f32[32,16384]{1,0:T(8,128)S(1)} fusion(f32[32,16384]{1,0:T(8,128)} %param.5, f32[32,256]{1,0:T(8,128)S(1)} %fusion.1, f32[256,16384]{1,0:T(8,128)} %all-gather.3.cloned.1.call-done), kind=kOutput, calls=%fused_computation.1 | convolution fusion | flops 1611137024 | bytes 21004288 | tf_op jit(solution)/shard_map/dot_general | solution.py:22
  133.6 0.0 copy-start.1
  133.6 25.0 %all-gather.5.cloned.1.call-done = f32[256,16384]{1,0:T(8,128)} async-done(((f32[8,16384]{1,0:T(8,128)}), f32[256,16384]{1,0:T(8,128)}) %all-gather.5.cloned.1.call-update) | async-done | bytes 16777232 | tf_op jit(solution)/shard_map/all_gather | solution.py:33
  158.6 17.1 %convolution_bitcast_fusion = f32[256,32]{0,1:T(8,128)S(1)} fusion(f32[32,16384]{1,0:T(8,128)S(1)} %convolution_subtract_fusion.1, f32[256,16384]{1,0:T(8,128)} %all-gather.5.cloned.1.call-done), kind=kOutput, calls=%fused_computation.2 | convolution fusion | flops 1610612736 | bytes 18907136 | tf_op jit(solution)/shard_map/dot_general | solution.py:12
  175.7 17.3 %psum.15 = f32[256,32]{0,1:T(8,128)S(1)} all-reduce(f32[256,32]{0,1:T(8,128)S(1)} %convolution_bitcast_fusion), channel_id=1, replica_groups=mesh['row'=4,'col'=32] {'row'}, use_global_device_ids=true, to_apply=%region_1.0 | all-reduce | flops 8192 | bytes 65536 | tf_op jit(solution)/shard_map/psum | solution.py:39
  193.0 0.0 copy-done.1
  193.0 0.3 fusion.2
  193.4 14.1 %convolution_subtract_fusion = f32[32,16384]{1,0:T(8,128)} fusion(f32[32,16384]{1,0:T(8,128)S(1)} %convolution_subtract_fusion.1, f32[32,256]{1,0:T(8,128)S(1)} %fusion.2, f32[256,16384]{1,0:T(8,128)} %all-gather.5.cloned.1.call-done), kind=kOutput, calls=%fused_computation | convolution fusion | flops 1611137024 | bytes 21004288 | tf_op jit(solution)/shard_map/dot_general | solution.py:22
Async XLA Ops:
  6.5 112.8 %copy-start = (f32[256,256]{1,0:T(8,128)S(1)}, f32[256,256]{1,0:T(8,128)}, u32[]{:S(2)}) copy-start(f32[256,256]{1,0:T(8,128)} %param.9) | copy-start | bytes 786436
  6.5 77.9 %all-gather.3.cloned.1.call-start = ((), (), s32[]{:S(2)}) async-start(), calls=%async_computation | async-start | bytes 17301504 | tf_op jit(solution)/shard_map/all_gather | solution.py:34
  7.3 151.4 %all-gather.5.cloned.1.call-start = ((), (), s32[]{:S(2)}) async-start(), calls=%async_computation.1 | async-start | bytes 17301504 | tf_op jit(solution)/shard_map/all_gather | solution.py:33
  133.6 59.4 %copy-start.1 = (f32[256,256]{1,0:T(8,128)S(1)}, f32[256,256]{1,0:T(8,128)}, u32[]{:S(2)}) copy-start(f32[256,256]{1,0:T(8,128)} %param.8) | copy-start | bytes 786436
Sparse Core Ops, SparseCore 0:
  9.6 74.7 all-gather.2
  86.7 71.8 all-gather.4
where the time goes:
time: 214 us
  waiting for transfers between devices  103 us (48%)
  matrix products  61.7 us (29%)
  blocking collectives  36.2 us (17%)
  between operations  13.5 us (6%)
    all_gather x1, waiting for transfers between devices, shards(): lax.all_gather(v_second, 'col', axis=0, tiled=True)  76.5 us
    psum x2, blocking collectives, shards(): summed = lax.psum(local_term, 'row')  36.2 us
    dot_general x2, matrix products, inner_last(): lax.dot_general(left, right, (((1,), (1,)), ((), ())), precision=lax.Prec...  33 us
    dot_general x2, matrix products, inner_first(): lax.dot_general(left, right, (((0,), (0,)), ((), ())), precision=lax.Prec...  28 us
    all_gather x1, waiting for transfers between devices, shards(): lax.all_gather(v_first, 'col', axis=0, tiled=True)  25 us
  transfers between devices with their start and end apart: 2, of which 2 were waited for; matrix products, arithmetic and copies ran while one was open for 14% of the time, Pallas kernels for 0%

commit v1 on v0

v1 whole, which is shorter than its diff:
```python
import jax
import jax.numpy as jnp
from jax import lax
from jax.experimental import pallas as pl
from jax.experimental.pallas import tpu as pltpu
from jax.sharding import PartitionSpec as P

MESH = pl.DeviceIdType.MESH
F32 = jnp.float32
BF16 = jnp.bfloat16
HIGHEST = lax.Precision.HIGHEST

SIDE = 4
HALF = 8192
PART = HALF // SIDE
MINE = 32
TILE = 1024
OFFSETS = (1, 3, 2)


def inner(left, right):
    return lax.dot_general(left, right, (((1,), (1,)), ((), ())), preferred_element_type=F32)


def inner_full(left, right):
    return lax.dot_general(
        left, right, (((1,), (1,)), ((), ())), precision=HIGHEST, preferred_element_type=F32
    )


def plain(left, right):
    return jnp.dot(left, right, preferred_element_type=F32)


def plain_full(left, right):
    return jnp.dot(left, right, precision=HIGHEST, preferred_element_type=F32)


def split(value):
    high = value.astype(BF16)
    return high, (value - high.astype(F32)).astype(BF16)


def three(product, left, right):
    return (
        product(left[0], right[1]) + product(left[1], right[0]) + product(left[0], right[0])
    )


def body(
    e_ref, v1_ref, v2_ref, t1_ref, t2_ref, out_ref,
    vbuf, vhigh, vlow, ebuf, obuf, t1, t2, nmat,
    psend, precv, zsend, zrecv, xbuf,
    gsend, grecv, gzrecv, gfull,
    loc_sem, own_sem,
    m1_s, m1_r, m2_s, m2_r, m3_s, m3_r, dd_s, dd_r, e_s, e_r,
    g_s, g_r, gz_s, gz_r, gp_s, gp_r,
    w_s, w_r, z_s, z_r, x_s, x_r, o_s, o_r,
):
    col = lax.axis_index("col")
    z = lax.axis_index("row")
    x, y, k = col // 8, (col // 2) % 4, col % 2
    ring = (x, y)
    cross = (y, x)

    def shift(at, by):
        return lax.rem(at + by, SIDE)

    def along_x(by):
        return (z, shift(x, by) * 8 + y * 2 + k)

    def along_y(by):
        return (z, x * 8 + shift(y, by) * 2 + k)

    def along_z(by):
        return (shift(z, by), col)

    partner = (z, x * 8 + y * 2 + (1 - k))
    ring_peer = (along_x, along_y)
    cross_peer = (along_y, along_x)

    sent = []

    def send(src, dst, s, r, device):
        copy = pltpu.make_async_remote_copy(
            src_ref=src, dst_ref=dst, send_sem=s, recv_sem=r, device_id=device, device_id_type=MESH
        )
        copy.start()
        sent.append(copy)
        return copy

    barrier = pltpu.get_barrier_semaphore()
    for by in OFFSETS:
        for peer in (along_x, along_y, along_z):
            pl.semaphore_signal(barrier, inc=1, device_id=peer(by), device_id_type=MESH)
    pl.semaphore_signal(barrier, inc=1, device_id=partner, device_id_type=MESH)

    local = []

    def bring(src, dst, sem):
        copy = pltpu.make_async_copy(src, dst, sem)
        copy.start()
        local.append(copy)
        return copy

    def columns(h, part):
        return pl.ds(pl.multiple_of(h * HALF + part * PART, PART), PART)

    panels = (v1_ref, v2_ref)
    own_v = [
        [bring(panels[p].at[:, columns(h, ring[h])], vbuf.at[h, p, x, y, k], loc_sem.at[2 * h + p]) for p in range(2)]
        for h in range(2)
    ]
    own_e = [bring(e_ref.at[:, columns(h, ring[h])], ebuf.at[h, ring[h]], loc_sem.at[4 + h]) for h in range(2)]
    own_t = [bring(t1_ref, t1, loc_sem.at[6]), bring(t2_ref, t2, loc_sem.at[7])]

    pl.semaphore_wait(barrier, 10)

    m1 = [[[None] * 2 for _ in OFFSETS] for _ in range(2)]
    for d, by in enumerate(OFFSETS):
        for h in range(2):
            for p in range(2):
                m1[h][d][p] = send(
                    panels[p].at[:, columns(h, shift(ring[h], by))],
                    vbuf.at[h, p, x, y, k],
                    m1_s.at[h, d, p], m1_r.at[h, d, p], ring_peer[h](by),
                )

    def chunk(h, p, at):
        return vbuf.at[h, p, :, at, k] if h == 0 else vbuf.at[h, p, at, :, k]

    m2 = [[[None] * 2 for _ in range(2)] for _ in range(2)]
    dd = [[], []]
    for h in range(2):
        for copy in own_v[h]:
            copy.wait()
        for d in range(3):
            for p in range(2):
                m1[h][d][p].wait_recv()
        for turn in range(2):
            for way, by in ((0, 1), (1, 3)):
                p = turn if way == 0 else 1 - turn
                m2[h][way][p] = send(
                    chunk(h, p, cross[h]), chunk(h, p, cross[h]), m2_s.at[h, way, p], m2_r.at[h, way, p], cross_peer[h](by)
                )
        for p in range(2):
            dd[h].append(send(chunk(h, p, cross[h]), chunk(h, p, cross[h]), dd_s.at[h, p], dd_r.at[h, p], partner))

    moved = [[None] * 3 for _ in range(2)]
    for d, by in enumerate(OFFSETS):
        for h in range(2):
            moved[h][d] = send(
                e_ref.at[:, columns(h, shift(ring[h], by))],
                ebuf.at[h, ring[h]],
                e_s.at[h, d], e_r.at[h, d], ring_peer[h](by),
            )

    m3 = [[None] * 2 for _ in range(2)]
    for turn in range(2):
        for h in range(2):
            for way, by in ((0, 1), (1, 3)):
                p = turn if way == 0 else 1 - turn
                came = shift(cross[h], 4 - by)
                m2[h][way][p].wait_recv()
                if turn == 0:
                    m3[h][way] = send(
                        chunk(h, p, came), chunk(h, p, came), m3_s.at[h, way], m3_r.at[h, way], cross_peer[h](by)
                    )
                at = 2 + 2 * way + p
                dd[h].append(send(chunk(h, p, came), chunk(h, p, came), dd_s.at[h, at], dd_r.at[h, at], partner))
    for h in range(2):
        far = shift(cross[h], 2)
        for way in range(2):
            m3[h][way].wait_recv()
            at = 6 + way
            dd[h].append(send(chunk(h, way, far), chunk(h, way, far), dd_s.at[h, at], dd_r.at[h, at], partner))

    for h in range(2):
        for copy in dd[h]:
            copy.wait_recv()

        def cut(i, carry):
            p, at_x, at_y = i // 16, (i // 4) % 4, i % 4
            rows = pl.ds(pl.multiple_of(i * 16, 16), 16)
            high, low = split(vbuf[h, p, at_x, at_y].reshape(16, PART))
            vhigh[h, rows, :] = high
            vlow[h, rows, :] = low
            return carry

        lax.fori_loop(0, 32, cut, 0)

    def vectors(h, p):
        rows = pl.ds(p * 256, 256)
        return vhigh[h, rows, :], vlow[h, rows, :]

    g = [[None] * 3 for _ in range(2)]
    for h in range(2):
        mine = vbuf[h, 0, :, y, k] if h == 0 else vbuf[h, 0, x, :, k]
        terms = three(inner, split(mine.reshape(32, PART)), vectors(h, 1))
        gsend[h] = terms.reshape(SIDE, 8, 256)
        for d, by in enumerate(OFFSETS):
            g[h][d] = send(
                gsend.at[h, shift(ring[h], by)], grecv.at[h, d], g_s.at[h, d], g_r.at[h, d], ring_peer[h](by)
            )
    total = gsend[0, x] + gsend[1, y]
    for h in range(2):
        for d in range(3):
            g[h][d].wait_recv()
            total = total + grecv[h, d]
    gzrecv[3] = total
    gz = [send(gzrecv.at[3], gzrecv.at[d], gz_s.at[d], gz_r.at[d], along_z(by)) for d, by in enumerate(OFFSETS)]
    for copy in gz:
        copy.wait_recv()
    gfull[x, y, k] = total + gzrecv[0] + gzrecv[1] + gzrecv[2]
    spread = [
        send(gfull.at[x, y, k], gfull.at[x, y, k], gp_s.at[d], gp_r.at[d], along_x(by)) for d, by in enumerate(OFFSETS)
    ]
    for copy in spread:
        copy.wait_recv()
    spread = [
        send(gfull.at[:, y, k], gfull.at[:, y, k], gp_s.at[3 + d], gp_r.at[3 + d], along_y(by))
        for d, by in enumerate(OFFSETS)
    ]
    for copy in spread:
        copy.wait_recv()
    send(gfull.at[:, :, k], gfull.at[:, :, k], gp_s.at[6], gp_r.at[6], partner).wait_recv()
    for copy in own_t:
        copy.wait()
    nmat[...] = plain_full(plain_full(t1[...], gfull[...].reshape(256, 256)), t2[...])

    w = [[None] * 3 for _ in range(2)]
    for h in range(2):
        own_e[h].wait()
        for d in range(3):
            moved[h][d].wait_recv()
        vecs = split(ebuf[h].reshape(SIDE * MINE, PART))
        for p in range(2):
            psend[h, :, :, pl.ds(p * 256, 256)] = three(inner, vecs, vectors(h, p)).reshape(SIDE, MINE, 256)
        for d, by in enumerate(OFFSETS):
            w[h][d] = send(
                psend.at[h, shift(ring[h], by)], precv.at[h, d], w_s.at[h, d], w_r.at[h, d], ring_peer[h](by)
            )
    total = psend[0, x] + psend[1, y]
    for h in range(2):
        for d in range(3):
            w[h][d].wait_recv()
            total = total + precv[h, d]
    zsend[...] = total
    zs = [send(zsend, zrecv.at[d], z_s.at[d], z_r.at[d], along_z(by)) for d, by in enumerate(OFFSETS)]
    for copy in zs:
        copy.wait_recv()
    total = total + zrecv[0] + zrecv[1] + zrecv[2]
    first, second = total[:, :256], total[:, 256:]
    coef_first = inner_full(first, t1[...]) - inner_full(second, nmat[...])
    coef_second = inner_full(second, t2[...])
    for h in range(2):
        xbuf[h, ring[h], :, pl.ds(0, 256)] = coef_first
        xbuf[h, ring[h], :, pl.ds(256, 256)] = coef_second
    xs = [[None] * 3 for _ in range(2)]
    for h in range(2):
        for d, by in enumerate(OFFSETS):
            xs[h][d] = send(
                xbuf.at[h, ring[h]], xbuf.at[h, ring[h]], x_s.at[h, d], x_r.at[h, d], ring_peer[h](by)
            )

    back = []
    for h in range(2):
        for d in range(3):
            xs[h][d].wait_recv()
        coefs = split(xbuf[h].reshape(SIDE * MINE, 512))
        for tile in range(PART // TILE):
            cols = pl.ds(tile * TILE, TILE)
            change = three(plain, coefs, (vhigh[h, :, cols], vlow[h, :, cols]))
            obuf[h, :, :, cols] = ebuf[h, :, :, cols] - change.reshape(SIDE, MINE, TILE)
            there = pl.ds(pl.multiple_of(h * HALF + ring[h] * PART + tile * TILE, TILE), TILE)
            for d, by in enumerate(OFFSETS):
                back.append(
                    send(
                        obuf.at[h, shift(ring[h], by), :, cols], out_ref.at[:, there],
                        o_s.at[h, tile, d], o_r.at[h, tile, d], ring_peer[h](by),
                    )
                )
            bring(obuf.at[h, ring[h], :, cols], out_ref.at[:, there], own_sem.at[h, tile]).wait()
    for copy in back:
        copy.wait_recv()
    for copy in sent:
        copy.wait_send()


def shards(evecs, v_first, v_second, t_first, t_second):
    vmem = pltpu.VMEM
    dma = pltpu.SemaphoreType.DMA
    tiles = PART // TILE

    def both(*shape):
        return [dma(shape), dma(shape)]

    return pl.pallas_call(
        body,
        out_shape=jax.ShapeDtypeStruct(evecs.shape, evecs.dtype),
        in_specs=[pl.BlockSpec(memory_space=pl.ANY)] * 5,
        out_specs=pl.BlockSpec(memory_space=pl.ANY),
        scratch_shapes=[
            vmem((2, 2, 4, 4, 2, 8, PART), F32),
            vmem((2, 512, PART), BF16),
            vmem((2, 512, PART), BF16),
            vmem((2, SIDE, MINE, PART), F32),
            vmem((2, SIDE, MINE, PART), F32),
            vmem((256, 256), F32),
            vmem((256, 256), F32),
            vmem((256, 256), F32),
            vmem((2, SIDE, MINE, 512), F32),
            vmem((2, 3, MINE, 512), F32),
            vmem((MINE, 512), F32),
            vmem((3, MINE, 512), F32),
            vmem((2, SIDE, MINE, 512), F32),
            vmem((2, SIDE, 8, 256), F32),
            vmem((2, 3, 8, 256), F32),
            vmem((4, 8, 256), F32),
            vmem((4, 4, 2, 8, 256), F32),
            dma((8,)),
            dma((2, tiles)),
            *both(2, 3, 2),
            *both(2, 2, 2),
            *both(2, 2),
            *both(2, 8),
            *both(2, 3),
            *both(2, 3),
            *both(3),
            *both(7),
            *both(2, 3),
            *both(3),
            *both(2, 3),
            *both(2, tiles, 3),
        ],
        compiler_params=pltpu.CompilerParams(
            collective_id=0, has_side_effects=True, vmem_limit_bytes=56 << 20
        ),
        name="back_transform",
    )(evecs, v_first, v_second, t_first, t_second)


def solution(mesh):
    placed = (P("col", "row"), P("col", "row"), P("col", "row"), P(), P())
    return jax.shard_map(
        shards, mesh=mesh, in_specs=placed, out_specs=P("col", "row"), check_vma=False
    )
```

time: 214 us -> 109 us (0.51)
  Pallas kernels: 0 us -> 106 us
  waiting for transfers between devices: 103 us -> 0 us
  matrix products: 61.7 us -> 0 us
  blocking collectives: 36.2 us -> 0 us
  between operations: 13.5 us -> 0.01 us
  local copies, waits for them, and re-layouts: 0.01 us -> 3.05 us
    pallas_call x0 -> x1, Pallas kernels: none -> 106 us  [shards(): pl.pallas_call(body, out_shape=jax.ShapeDtypeStruct(evecs.shape, evecs.dt...]
    all_gather x2 -> x0, waiting for transfers between devices: 102 us -> none  [the longest x1 76.5 us: shards(): lax.all_gather(v_second, 'col', axis=0, tiled=True)]
    dot_general x6 -> x0, matrix products: 61.7 us -> none  [the longest x2 33 us: inner_last(): lax.dot_general(left, right, (((1,), (1,)), ((), ())), precision=lax.Prec...]
    psum x2 -> x0, blocking collectives: 36.2 us -> none  [shards(): summed = lax.psum(local_term, 'row')]
    unnamed x4 -> x1, local copies, waits for them, and re-layouts: 0.01 us -> 3.05 us
  transfers between devices with their start and end apart: 2 -> 0, of which waited for: 2 -> 0; matrix products, arithmetic and copies ran while one was open for 14% -> 0% of each run, Pallas kernels for 0% -> 0%
where the time goes in v1:
time: 109 us
  Pallas kernels  106 us (97%)
  local copies, waits for them, and re-layouts  3.05 us (3%)
    pallas_call x1, Pallas kernels, shards(): pl.pallas_call(body, out_shape=jax.ShapeDtypeStruct(evecs.shape, evecs.dt...  106 us
    unnamed x1, local copies, waits for them, and re-layouts  3.05 us

profile of v1, /device:TPU:0, one launch (start us, length us, event | category | flops | bytes accessed | tf_op | source)
XLA Modules:
  0.0 109.2 jit_solution(955723640131870688)
XLA Ops:
  0.0 106.2 %back_transform.1 = f32[32,16384]{1,0:T(8,128)} custom-call(f32[32,16384]{1,0:T(8,128)} %e_ref.1, f32[8,16384]{1,0:T(8,128)} %v1_ref.1, f32[8,16384]{1,0:T(8,128)} %v2_ref.1, f32[256,256]{1,0:T(8,128)} %t1_ref.1, f32[256,256]{1,0:T(8,128)} %t2_ref.1), custom_call_target="tpu_custom_call" | custom-call | tf_op jit(solution)/shard_map/back_transform/pallas_call | solution.py:298
  106.2 3.0 %copy.7 = f32[32,16384]{1,0:T(8,128)} copy(f32[32,16384]{1,0:T(8,128)} %back_transform.1) | data formatting | bytes 4194304

commit v2 on v0

v2 whole, which is shorter than its diff:
```python
import jax
import jax.numpy as jnp
from jax import lax
from jax.experimental import pallas as pl
from jax.experimental.pallas import tpu as pltpu
from jax.sharding import PartitionSpec as P

MESH = pl.DeviceIdType.MESH
F32 = jnp.float32
BF16 = jnp.bfloat16
HIGHEST = lax.Precision.HIGHEST

SIDE = 4
HALF = 8192
PART = HALF // SIDE
MINE = 32
CHUNKS = 2
ROWS = MINE // CHUNKS
TILE = 1024
TILES = PART // TILE
OFFSETS = (1, 3, 2)
WAYS = ((0, 1), (1, 3))


def inner(left, right):
    return lax.dot_general(left, right, (((1,), (1,)), ((), ())), preferred_element_type=F32)


def inner_full(left, right):
    return lax.dot_general(
        left, right, (((1,), (1,)), ((), ())), precision=HIGHEST, preferred_element_type=F32
    )


def plain(left, right):
    return jnp.dot(left, right, preferred_element_type=F32)


def plain_full(left, right):
    return jnp.dot(left, right, precision=HIGHEST, preferred_element_type=F32)


def split(value):
    high = value.astype(BF16)
    return high, (value - high.astype(F32)).astype(BF16)


def products_of(vectors, rows):
    count = rows[0].shape[0]
    high = inner(vectors[0], jnp.concatenate(rows, axis=0))
    return (high[:, :count] + high[:, count:] + inner(vectors[1], rows[0])).T


def combine(coefs, vectors):
    count = coefs[0].shape[0]
    high = plain(jnp.concatenate(coefs, axis=0), vectors[0])
    return high[:count] + high[count:] + plain(coefs[0], vectors[1])


def body(
    e_ref, v1_ref, v2_ref, t1_ref, t2_ref, out_ref,
    vbuf, vhigh, vlow, ebuf, obuf, t1, t2, nmat,
    psend, precv, zsend, zrecv, xbuf,
    gsend, grecv, gpart, gfull,
    loc_sem, own_sem,
    m1_s, m1_r, m2_s, m2_r, m3_s, m3_r, dd_s, dd_r, e_s, e_r,
    g_s, g_r, gz_s, gz_r, gp_s, gp_r,
    w_s, w_r, z_s, z_r, x_s, x_r, o_s, o_r,
):
    col = lax.axis_index("col")
    z = lax.axis_index("row")
    x, y, k = col // 8, (col // 2) % 4, col % 2
    ring = (x, y)
    cross = (y, x)

    def shift(at, by):
        return lax.rem(at + by, SIDE)

    def device(dx=0, dy=0, dz=0, dk=0):
        return (shift(z, dz), shift(x, dx) * 8 + shift(y, dy) * 2 + lax.rem(k + dk, 2))

    def along_x(by):
        return device(dx=by)

    def along_y(by):
        return device(dy=by)

    def along_z(by):
        return device(dz=by)

    partner = device(dk=1)
    ring_peer = (along_x, along_y)
    cross_peer = (along_y, along_x)

    sent = []

    def send(src, dst, s, r, to):
        copy = pltpu.make_async_remote_copy(
            src_ref=src, dst_ref=dst, send_sem=s, recv_sem=r, device_id=to, device_id_type=MESH
        )
        copy.start()
        sent.append(copy)
        return copy

    barrier = pltpu.get_barrier_semaphore()
    row_peers = [(dx, dz) for dz in (0, *OFFSETS) for dx in (0, *OFFSETS) if dx or dz]
    col_peers = [(dy, dk) for dk in (0, 1) for dy in (0, *OFFSETS) if dy or dk]
    peers = [device(dx=dx, dz=dz) for dx, dz in row_peers] + [device(dy=dy, dk=dk) for dy, dk in col_peers]
    for peer in peers:
        pl.semaphore_signal(barrier, inc=1, device_id=peer, device_id_type=MESH)

    def bring(src, dst, sem):
        copy = pltpu.make_async_copy(src, dst, sem)
        copy.start()
        return copy

    def columns(h, part):
        return pl.ds(pl.multiple_of(h * HALF + part * PART, PART), PART)

    def rows(c):
        return pl.ds(c * ROWS, ROWS)

    panels = (v1_ref, v2_ref)
    both = range(2)
    own_v = [
        [bring(panels[p].at[:, columns(h, ring[h])], vbuf.at[h, p, x, y, k], loc_sem.at[2 * h + p]) for p in both]
        for h in both
    ]
    own_e = [
        [bring(e_ref.at[rows(c), columns(h, ring[h])], ebuf.at[h, c, ring[h]], loc_sem.at[4 + 2 * c + h]) for h in both]
        for c in range(CHUNKS)
    ]
    at_t = 4 + 2 * CHUNKS
    own_t = [bring(t1_ref, t1, loc_sem.at[at_t]), bring(t2_ref, t2, loc_sem.at[at_t + 1])]

    pl.semaphore_wait(barrier, len(peers))

    m1 = [[None] * 3 for _ in both]
    for d, by in enumerate(OFFSETS):
        for h in both:
            m1[h][d] = [
                send(
                    panels[p].at[:, columns(h, shift(ring[h], by))],
                    vbuf.at[h, p, x, y, k],
                    m1_s.at[h, d, p], m1_r.at[h, d, p], ring_peer[h](by),
                )
                for p in both
            ]

    def piece(h, j, at):
        origin = ring[h] if j == 0 else shift(ring[h], 4 - OFFSETS[j - 1])
        return vbuf.at[h, :, origin, at, k] if h == 0 else vbuf.at[h, :, at, origin, k]

    m2 = [[[None] * 4 for _ in both] for _ in both]
    m3 = [[[None] * 4 for _ in both] for _ in both]
    dd = [[None] * 20 for _ in both]

    def mirror(h, src, at):
        dd[h][at] = send(src, src, dd_s.at[h, at], dd_r.at[h, at], partner)

    def cut(h, j, at, copies):
        origin = ring[h] if j == 0 else shift(ring[h], 4 - OFFSETS[j - 1])
        at_x, at_y = (origin, at) if h == 0 else (at, origin)
        for copy in copies:
            dd[h][copy].wait_recv()
        for p in both:
            to = pl.ds(pl.multiple_of(p * 256 + at_x * 64 + at_y * 16, 16), 16)
            vhigh[h, to, :], vlow[h, to, :] = split(vbuf[h, p, at_x, at_y].reshape(16, PART))

    def pass_on(h, j):
        src = piece(h, j, cross[h])
        for way, by in WAYS:
            m2[h][way][j] = send(src, src, m2_s.at[h, way, j], m2_r.at[h, way, j], cross_peer[h](by))
        mirror(h, src, j)

    def pass_further(h, j):
        for way, by in WAYS:
            m2[h][way][j].wait_recv()
            src = piece(h, j, shift(cross[h], 4 - by))
            part = src.at[way]
            m3[h][way][j] = send(part, part, m3_s.at[h, way, j], m3_r.at[h, way, j], cross_peer[h](by))
            mirror(h, src, 4 + 4 * way + j)

    def finish(h, j):
        for way, _ in WAYS:
            m3[h][way][j].wait_recv()
            mirror(h, piece(h, j, shift(cross[h], 2)).at[way], 12 + 4 * way + j)

    def arrived(h, d):
        for p in both:
            m1[h][d][p].wait_recv()
        pass_on(h, d + 1)

    moved = [[[None] * 3 for _ in both] for _ in range(CHUNKS)]

    def move(c):
        for d, by in enumerate(OFFSETS):
            for h in both:
                moved[c][h][d] = send(
                    e_ref.at[rows(c), columns(h, shift(ring[h], by))],
                    ebuf.at[h, c, ring[h]],
                    e_s.at[c, h, d], e_r.at[c, h, d], ring_peer[h](by),
                )

    def cut_near(j):
        for h in both:
            cut(h, j, cross[h], [j])

    def cut_next(j):
        for h in both:
            for way, by in WAYS:
                cut(h, j, shift(cross[h], 4 - by), [4 + 4 * way + j])

    def cut_far(j):
        for h in both:
            cut(h, j, shift(cross[h], 2), [12 + j, 16 + j])

    for h in both:
        for copy in own_v[h]:
            copy.wait()
        pass_on(h, 0)
    for d in (0, 1):
        for h in both:
            arrived(h, d)
    for h in both:
        pass_further(h, 0)
    for h in both:
        arrived(h, 2)
    cut_near(0)
    cut_near(1)
    cut_near(2)
    for h in both:
        pass_further(h, 1)
    cut_near(3)
    for h in both:
        pass_further(h, 2)
    cut_next(0)
    cut_next(1)
    for h in both:
        pass_further(h, 3)
    move(0)
    move(1)
    for h in both:
        finish(h, 0)
    cut_next(2)
    for h in both:
        finish(h, 1)
    cut_next(3)
    for h in both:
        finish(h, 2)
    cut_far(0)
    for h in both:
        finish(h, 3)
    cut_far(1)
    cut_far(2)
    cut_far(3)

    g = [[None] * 3 for _ in both]
    for h in both:
        mine = vbuf[h, 0, :, y, k] if h == 0 else vbuf[h, 0, x, :, k]
        terms = products_of((vhigh[h, pl.ds(256, 256), :], vlow[h, pl.ds(256, 256), :]), split(mine.reshape(32, PART)))
        gsend[h] = terms.reshape(SIDE, 8, 256)
        for d, by in enumerate(OFFSETS):
            g[h][d] = send(
                gsend.at[h, shift(ring[h], by)], grecv.at[h, d], g_s.at[h, d], g_r.at[h, d], ring_peer[h](by)
            )

    def gram_rows():
        total = gsend[0, x] + gsend[1, y]
        for h in both:
            for d in range(3):
                g[h][d].wait_recv()
                total = total + grecv[h, d]
        gpart[z, x] = total
        mine = gpart.at[z, x]
        return [
            send(mine, mine, gz_s.at[i], gz_r.at[i], device(dx=dx, dz=dz)) for i, (dx, dz) in enumerate(row_peers)
        ]

    def gram_sum(copies):
        for copy in copies:
            copy.wait_recv()
        gfull[:, y, k] = gpart[0] + gpart[1] + gpart[2] + gpart[3]
        mine = gfull.at[:, y, k]
        return [
            send(mine, mine, gp_s.at[i], gp_r.at[i], device(dy=dy, dk=dk)) for i, (dy, dk) in enumerate(col_peers)
        ]

    def gram_use(copies):
        for copy in copies:
            copy.wait_recv()
        for copy in own_t:
            copy.wait()
        nmat[...] = plain_full(plain_full(t1[...], gfull[...].reshape(256, 256)), t2[...])

    w = [[[None] * 3 for _ in both] for _ in range(CHUNKS)]
    zs = [None] * CHUNKS
    xs = [[[None] * 3 for _ in both] for _ in range(CHUNKS)]
    back = []

    def products(c):
        for h in both:
            own_e[c][h].wait()
            for d in range(3):
                moved[c][h][d].wait_recv()
            vecs = split(ebuf[h, c].reshape(SIDE * ROWS, PART))
            psend[h, c] = products_of((vhigh[h], vlow[h]), vecs).reshape(SIDE, ROWS, 512)
            for d, by in enumerate(OFFSETS):
                w[c][h][d] = send(
                    psend.at[h, c, shift(ring[h], by)],
                    precv.at[c, h, d], w_s.at[c, h, d], w_r.at[c, h, d], ring_peer[h](by),
                )

    def plane_sum(c):
        total = psend[0, c, x] + psend[1, c, y]
        for h in both:
            for d in range(3):
                w[c][h][d].wait_recv()
                total = total + precv[c, h, d]
        zsend[c] = total
        zs[c] = [
            send(zsend.at[c], zrecv.at[c, d], z_s.at[c, d], z_r.at[c, d], along_z(by)) for d, by in enumerate(OFFSETS)
        ]

    def coefficients(c):
        total = zsend[c]
        for d in range(3):
            zs[c][d].wait_recv()
            total = total + zrecv[c, d]
        first, second = total[:, :256], total[:, 256:]
        coef_first = inner_full(first, t1[...]) - inner_full(second, nmat[...])
        coef_second = inner_full(second, t2[...])
        for h in both:
            xbuf[h, c, ring[h], :, pl.ds(0, 256)] = coef_first
            xbuf[h, c, ring[h], :, pl.ds(256, 256)] = coef_second
        for h in both:
            mine = xbuf.at[h, c, ring[h]]
            for d, by in enumerate(OFFSETS):
                xs[c][h][d] = send(mine, mine, x_s.at[c, h, d], x_r.at[c, h, d], ring_peer[h](by))

    def update(c):
        for h in both:
            for d in range(3):
                xs[c][h][d].wait_recv()
            coefs = split(xbuf[h, c].reshape(SIDE * ROWS, 512))
            for tile in range(TILES):
                cols = pl.ds(tile * TILE, TILE)
                change = combine(coefs, (vhigh[h, :, cols], vlow[h, :, cols]))
                obuf[h, c, :, :, cols] = ebuf[h, c, :, :, cols] - change.reshape(SIDE, ROWS, TILE)
                there = pl.ds(pl.multiple_of(h * HALF + ring[h] * PART + tile * TILE, TILE), TILE)
                for d, by in enumerate(OFFSETS):
                    back.append(
                        send(
                            obuf.at[h, c, shift(ring[h], by), :, cols], out_ref.at[rows(c), there],
                            o_s.at[c, h, tile, d], o_r.at[c, h, tile, d], ring_peer[h](by),
                        )
                    )
                stays.append(bring(obuf.at[h, c, ring[h], :, cols], out_ref.at[rows(c), there], own_sem.at[c, h, tile]))

    stays = []
    products(0)
    step = gram_rows()
    products(1)
    plane_sum(0)
    step = gram_sum(step)
    plane_sum(1)
    gram_use(step)
    coefficients(0)
    coefficients(1)
    update(0)
    update(1)
    for copy in back:
        copy.wait_recv()
    for copy in stays:
        copy.wait()
    for copy in sent:
        copy.wait_send()


def shards(evecs, v_first, v_second, t_first, t_second):
    vmem = pltpu.VMEM
    dma = pltpu.SemaphoreType.DMA

    def both(*shape):
        return [dma(shape), dma(shape)]

    return pl.pallas_call(
        body,
        out_shape=jax.ShapeDtypeStruct(evecs.shape, evecs.dtype),
        in_specs=[pl.BlockSpec(memory_space=pl.ANY)] * 5,
        out_specs=pl.BlockSpec(memory_space=pl.ANY),
        scratch_shapes=[
            vmem((2, 2, 4, 4, 2, 8, PART), F32),
            vmem((2, 512, PART), BF16),
            vmem((2, 512, PART), BF16),
            vmem((2, CHUNKS, SIDE, ROWS, PART), F32),
            vmem((2, CHUNKS, SIDE, ROWS, PART), F32),
            vmem((256, 256), F32),
            vmem((256, 256), F32),
            vmem((256, 256), F32),
            vmem((2, CHUNKS, SIDE, ROWS, 512), F32),
            vmem((CHUNKS, 2, 3, ROWS, 512), F32),
            vmem((CHUNKS, ROWS, 512), F32),
            vmem((CHUNKS, 3, ROWS, 512), F32),
            vmem((2, CHUNKS, SIDE, ROWS, 512), F32),
            vmem((2, SIDE, 8, 256), F32),
            vmem((2, 3, 8, 256), F32),
            vmem((4, 4, 8, 256), F32),
            vmem((4, 4, 2, 8, 256), F32),
            dma((6 + 2 * CHUNKS,)),
            dma((CHUNKS, 2, TILES)),
            *both(2, 3, 2),
            *both(2, 2, 4),
            *both(2, 2, 4),
            *both(2, 20),
            *both(CHUNKS, 2, 3),
            *both(2, 3),
            *both(15),
            *both(7),
            *both(CHUNKS, 2, 3),
            *both(CHUNKS, 3),
            *both(CHUNKS, 2, 3),
            *both(CHUNKS, 2, TILES, 3),
        ],
        compiler_params=pltpu.CompilerParams(
            collective_id=0, has_side_effects=True, vmem_limit_bytes=56 << 20
        ),
        name="back_transform",
    )(evecs, v_first, v_second, t_first, t_second)


def solution(mesh):
    placed = (P("col", "row"), P("col", "row"), P("col", "row"), P(), P())
    return jax.shard_map(
        shards, mesh=mesh, in_specs=placed, out_specs=P("col", "row"), check_vma=False
    )
```

time: 214 us -> 82.7 us (0.39)
  waiting for transfers between devices: 103 us -> 0 us
  Pallas kernels: 0 us -> 79.5 us
  matrix products: 61.7 us -> 0 us
  blocking collectives: 36.2 us -> 0 us
  between operations: 13.5 us -> 0.01 us
  local copies, waits for them, and re-layouts: 0.01 us -> 3.05 us
    all_gather x2 -> x0, waiting for transfers between devices: 102 us -> none  [the longest x1 76.5 us: shards(): lax.all_gather(v_second, 'col', axis=0, tiled=True)]
    pallas_call x0 -> x1, Pallas kernels: none -> 79.5 us  [shards(): pl.pallas_call(body, out_shape=jax.ShapeDtypeStruct(evecs.shape, evecs.dt...]
    dot_general x6 -> x0, matrix products: 61.7 us -> none  [the longest x2 33 us: inner_last(): lax.dot_general(left, right, (((1,), (1,)), ((), ())), precision=lax.Prec...]
    psum x2 -> x0, blocking collectives: 36.2 us -> none  [shards(): summed = lax.psum(local_term, 'row')]
    unnamed x4 -> x1, local copies, waits for them, and re-layouts: 0.01 us -> 3.05 us
  transfers between devices with their start and end apart: 2 -> 0, of which waited for: 2 -> 0; matrix products, arithmetic and copies ran while one was open for 14% -> 0% of each run, Pallas kernels for 0% -> 0%
where the time goes in v2:
time: 82.7 us; the launch traced here: 82.6 us
  Pallas kernels  79.5 us (96%)
  local copies, waits for them, and re-layouts  3.05 us (4%)
    pallas_call x1, Pallas kernels, shards(): pl.pallas_call(body, out_shape=jax.ShapeDtypeStruct(evecs.shape, evecs.dt...  79.5 us
    unnamed x1, local copies, waits for them, and re-layouts  3.05 us

profile of v2, /device:TPU:0, one launch (start us, length us, event | category | flops | bytes accessed | tf_op | source)
XLA Modules:
  0.0 82.6 jit_solution(3658629423934621094)
XLA Ops:
  0.0 79.5 %back_transform.1 = f32[32,16384]{1,0:T(8,128)} custom-call(f32[32,16384]{1,0:T(8,128)} %e_ref.1, f32[8,16384]{1,0:T(8,128)} %v1_ref.1, f32[8,16384]{1,0:T(8,128)} %v2_ref.1, f32[256,256]{1,0:T(8,128)} %t1_ref.1, f32[256,256]{1,0:T(8,128)} %t2_ref.1), custom_call_target="tpu_custom_call" | custom-call | tf_op jit(solution)/shard_map/back_transform/pallas_call | solution.py:387
  79.5 3.0 %copy.7 = f32[32,16384]{1,0:T(8,128)} copy(f32[32,16384]{1,0:T(8,128)} %back_transform.1) | data formatting | bytes 4194304

commit v3 on v2

--- a/solution.py
+++ b/solution.py
@@ -48,7 +48,7 @@
 def products_of(vectors, rows):
     count = rows[0].shape[0]
     high = inner(vectors[0], jnp.concatenate(rows, axis=0))
-    return (high[:, :count] + high[:, count:] + inner(vectors[1], rows[0])).T
+    return high[:, :count] + high[:, count:] + inner(vectors[1], rows[0])
 
 
 def combine(coefs, vectors):
@@ -59,7 +59,7 @@
 
 def body(
     e_ref, v1_ref, v2_ref, t1_ref, t2_ref, out_ref,
-    vbuf, vhigh, vlow, ebuf, obuf, t1, t2, nmat,
+    vbuf, vhigh, vlow, ebuf, obuf, t1, t2, t1_gram,
     psend, precv, zsend, zrecv, xbuf,
     gsend, grecv, gpart, gfull,
     loc_sem, own_sem,
@@ -103,9 +103,7 @@
         return copy
 
     barrier = pltpu.get_barrier_semaphore()
-    row_peers = [(dx, dz) for dz in (0, *OFFSETS) for dx in (0, *OFFSETS) if dx or dz]
-    col_peers = [(dy, dk) for dk in (0, 1) for dy in (0, *OFFSETS) if dy or dk]
-    peers = [device(dx=dx, dz=dz) for dx, dz in row_peers] + [device(dy=dy, dk=dk) for dy, dk in col_peers]
+    peers = [along(by) for along in (along_x, along_y, along_z) for by in OFFSETS] + [partner]
     for peer in peers:
         pl.semaphore_signal(barrier, inc=1, device_id=peer, device_id_type=MESH)
 
@@ -238,10 +236,9 @@
     cut_next(1)
     for h in both:
         pass_further(h, 3)
+    for h in both:
+        finish(h, 0)
     move(0)
-    move(1)
-    for h in both:
-        finish(h, 0)
     cut_next(2)
     for h in both:
         finish(h, 1)
@@ -259,7 +256,7 @@
     for h in both:
         mine = vbuf[h, 0, :, y, k] if h == 0 else vbuf[h, 0, x, :, k]
         terms = products_of((vhigh[h, pl.ds(256, 256), :], vlow[h, pl.ds(256, 256), :]), split(mine.reshape(32, PART)))
-        gsend[h] = terms.reshape(SIDE, 8, 256)
+        gsend[h] = terms.T.reshape(SIDE, 8, 256)
         for d, by in enumerate(OFFSETS):
             g[h][d] = send(
                 gsend.at[h, shift(ring[h], by)], grecv.at[h, d], g_s.at[h, d], g_r.at[h, d], ring_peer[h](by)
@@ -273,25 +270,31 @@
                 total = total + grecv[h, d]
         gpart[z, x] = total
         mine = gpart.at[z, x]
-        return [
-            send(mine, mine, gz_s.at[i], gz_r.at[i], device(dx=dx, dz=dz)) for i, (dx, dz) in enumerate(row_peers)
-        ]
+        return [send(mine, mine, gz_s.at[d], gz_r.at[d], along_z(by)) for d, by in enumerate(OFFSETS)]
+
+    def gram_spread(copies):
+        for copy in copies:
+            copy.wait_recv()
+        gfull[x, y, k] = gpart[0, x] + gpart[1, x] + gpart[2, x] + gpart[3, x]
+        mine = gfull.at[x, y, k]
+        return [send(mine, mine, gz_s.at[3 + d], gz_r.at[3 + d], along_x(by)) for d, by in enumerate(OFFSETS)]
 
     def gram_sum(copies):
         for copy in copies:
             copy.wait_recv()
-        gfull[:, y, k] = gpart[0] + gpart[1] + gpart[2] + gpart[3]
         mine = gfull.at[:, y, k]
-        return [
-            send(mine, mine, gp_s.at[i], gp_r.at[i], device(dy=dy, dk=dk)) for i, (dy, dk) in enumerate(col_peers)
-        ]
+        return [send(mine, mine, gp_s.at[d], gp_r.at[d], along_y(by)) for d, by in enumerate(OFFSETS)]
+
+    def gram_partner(copies):
+        for copy in copies:
+            copy.wait_recv()
+        mine = gfull.at[:, :, k]
+        return [send(mine, mine, gp_s.at[3], gp_r.at[3], partner)]
 
     def gram_use(copies):
         for copy in copies:
             copy.wait_recv()
-        for copy in own_t:
-            copy.wait()
-        nmat[...] = plain_full(plain_full(t1[...], gfull[...].reshape(256, 256)), t2[...])
+        t1_gram[...] = plain_full(t1[...], gfull[...].reshape(256, 256))
 
     w = [[[None] * 3 for _ in both] for _ in range(CHUNKS)]
     zs = [None] * CHUNKS
@@ -299,12 +302,15 @@
     back = []
 
     def products(c):
+        terms = []
         for h in both:
             own_e[c][h].wait()
             for d in range(3):
                 moved[c][h][d].wait_recv()
             vecs = split(ebuf[h, c].reshape(SIDE * ROWS, PART))
-            psend[h, c] = products_of((vhigh[h], vlow[h]), vecs).reshape(SIDE, ROWS, 512)
+            terms.append(products_of((vhigh[h], vlow[h]), vecs))
+        psend[:, c] = jnp.concatenate(terms, axis=1).T.reshape(2, SIDE, ROWS, 512)
+        for h in both:
             for d, by in enumerate(OFFSETS):
                 w[c][h][d] = send(
                     psend.at[h, c, shift(ring[h], by)],
@@ -324,12 +330,14 @@
 
     def coefficients(c):
         total = zsend[c]
+        for copy in own_t if c == 0 else []:
+            copy.wait()
         for d in range(3):
             zs[c][d].wait_recv()
             total = total + zrecv[c, d]
         first, second = total[:, :256], total[:, 256:]
-        coef_first = inner_full(first, t1[...]) - inner_full(second, nmat[...])
         coef_second = inner_full(second, t2[...])
+        coef_first = inner_full(first, t1[...])
         for h in both:
             xbuf[h, c, ring[h], :, pl.ds(0, 256)] = coef_first
             xbuf[h, c, ring[h], :, pl.ds(256, 256)] = coef_second
@@ -342,7 +350,9 @@
         for h in both:
             for d in range(3):
                 xs[c][h][d].wait_recv()
-            coefs = split(xbuf[h, c].reshape(SIDE * ROWS, 512))
+            first, second = (xbuf[h, c, :, :, pl.ds(p * 256, 256)].reshape(SIDE * ROWS, 256) for p in both)
+            first = first - inner_full(second, t1_gram[...])
+            coefs = split(jnp.concatenate([first, second], axis=1))
             for tile in range(TILES):
                 cols = pl.ds(tile * TILE, TILE)
                 change = combine(coefs, (vhigh[h, :, cols], vlow[h, :, cols]))
@@ -358,14 +368,17 @@
                 stays.append(bring(obuf.at[h, c, ring[h], :, cols], out_ref.at[rows(c), there], own_sem.at[c, h, tile]))
 
     stays = []
+    move(1)
     products(0)
     step = gram_rows()
+    plane_sum(0)
+    step = gram_spread(step)
     products(1)
-    plane_sum(0)
     step = gram_sum(step)
+    coefficients(0)
     plane_sum(1)
+    step = gram_partner(step)
     gram_use(step)
-    coefficients(0)
     coefficients(1)
     update(0)
     update(1)
@@ -377,6 +390,19 @@
         copy.wait_send()
 
 
+def hand_over(src, dst, held, sems):
+    spots = [(pl.ds(i * 8, 8), pl.ds(j * 8192, 8192)) for i in range(4) for j in range(2)]
+    arriving = [pltpu.make_async_copy(src.at[spot], held.at[spot], sems.at[0, i]) for i, spot in enumerate(spots)]
+    leaving = [pltpu.make_async_copy(held.at[spot], dst.at[spot], sems.at[1, i]) for i, spot in enumerate(spots)]
+    for copy in arriving:
+        copy.start()
+    for came, copy in zip(arriving, leaving):
+        came.wait()
+        copy.start()
+    for copy in leaving:
+        copy.wait()
+
+
 def shards(evecs, v_first, v_second, t_first, t_second):
     vmem = pltpu.VMEM
     dma = pltpu.SemaphoreType.DMA
@@ -384,7 +410,7 @@
     def both(*shape):
         return [dma(shape), dma(shape)]
 
-    return pl.pallas_call(
+    basis = pl.pallas_call(
         body,
         out_shape=jax.ShapeDtypeStruct(evecs.shape, evecs.dtype),
         in_specs=[pl.BlockSpec(memory_space=pl.ANY)] * 5,
@@ -415,8 +441,8 @@
             *both(2, 20),
             *both(CHUNKS, 2, 3),
             *both(2, 3),
-            *both(15),
-            *both(7),
+            *both(6),
+            *both(4),
             *both(CHUNKS, 2, 3),
             *both(CHUNKS, 3),
             *both(CHUNKS, 2, 3),
@@ -427,6 +453,15 @@
         ),
         name="back_transform",
     )(evecs, v_first, v_second, t_first, t_second)
+    return pl.pallas_call(
+        hand_over,
+        out_shape=jax.ShapeDtypeStruct(evecs.shape, evecs.dtype),
+        in_specs=[pl.BlockSpec(memory_space=pl.ANY)],
+        out_specs=pl.BlockSpec(memory_space=pl.ANY),
+        scratch_shapes=[vmem(evecs.shape, F32), dma((2, 8))],
+        compiler_params=pltpu.CompilerParams(vmem_limit_bytes=56 << 20),
+        name="hand_over",
+    )(basis)
 
 
 def solution(mesh):

time: 82.7 us -> 79 us (0.955)
  local copies, waits for them, and re-layouts: 3.05 us -> 0 us
    pallas_call x1, Pallas kernels: 79.5 us -> 76.3 us  [shards(): pl.pallas_call(body, out_shape=jax.ShapeDtypeStruct(evecs.shape, evecs.dt...]
    unnamed x1 -> x0, local copies, waits for them, and re-layouts: 3.05 us -> none
    pallas_call x0 -> x1, Pallas kernels: none -> 2.4 us  [shards(): pl.pallas_call(hand_over, out_shape=jax.ShapeDtypeStruct(evecs.shape, eve...]
where the time goes in v3:
time: 79 us; the launch traced here: 78.8 us
  Pallas kernels  78.7 us (100%)
    pallas_call x1, Pallas kernels, shards(): pl.pallas_call(body, out_shape=jax.ShapeDtypeStruct(evecs.shape, evecs.dt...  76.3 us
    pallas_call x1, Pallas kernels, shards(): pl.pallas_call(hand_over, out_shape=jax.ShapeDtypeStruct(evecs.shape, eve...  2.4 us

profile of v3, /device:TPU:0, one launch (start us, length us, event | category | flops | bytes accessed | tf_op | source)
XLA Modules:
  0.0 78.8 jit_solution(861336838246864584)
XLA Ops:
  0.0 76.3 %back_transform.1.src = f32[32,16384]{1,0:T(8,128)} custom-call(f32[32,16384]{1,0:T(8,128)} %e_ref.1, f32[8,16384]{1,0:T(8,128)} %v1_ref.1, f32[8,16384]{1,0:T(8,128)} %v2_ref.1, f32[256,256]{1,0:T(8,128)} %t1_ref.1, f32[256,256]{1,0:T(8,128)} %t2_ref.1), custom_call_target="tpu_custom_call" | custom-call | tf_op jit(solution)/shard_map/back_transform/pallas_call | solution.py:413
  76.3 2.4 %hand_over.1 = f32[32,16384]{1,0:T(8,128)} custom-call(f32[32,16384]{1,0:T(8,128)} %back_transform.1.src), custom_call_target="tpu_custom_call" | custom-call | tf_op jit(solution)/shard_map/hand_over/pallas_call | solution.py:456

commit v4 on v3

--- a/solution.py
+++ b/solution.py
@@ -14,8 +14,9 @@
 HALF = 8192
 PART = HALF // SIDE
 MINE = 32
-CHUNKS = 2
-ROWS = MINE // CHUNKS
+SIZES = (16, 16)
+STARTS = tuple(sum(SIZES[:c]) for c in range(len(SIZES)))
+CHUNKS = len(SIZES)
 TILE = 1024
 TILES = PART // TILE
 OFFSETS = (1, 3, 2)
@@ -116,7 +117,7 @@
         return pl.ds(pl.multiple_of(h * HALF + part * PART, PART), PART)
 
     def rows(c):
-        return pl.ds(c * ROWS, ROWS)
+        return pl.ds(STARTS[c], SIZES[c])
 
     panels = (v1_ref, v2_ref)
     both = range(2)
@@ -125,7 +126,7 @@
         for h in both
     ]
     own_e = [
-        [bring(e_ref.at[rows(c), columns(h, ring[h])], ebuf.at[h, c, ring[h]], loc_sem.at[4 + 2 * c + h]) for h in both]
+        [bring(e_ref.at[rows(c), columns(h, ring[h])], ebuf.at[h, ring[h], rows(c)], loc_sem.at[4 + 2 * c + h]) for h in both]
         for c in range(CHUNKS)
     ]
     at_t = 4 + 2 * CHUNKS
@@ -196,7 +197,7 @@
             for h in both:
                 moved[c][h][d] = send(
                     e_ref.at[rows(c), columns(h, shift(ring[h], by))],
-                    ebuf.at[h, c, ring[h]],
+                    ebuf.at[h, ring[h], rows(c)],
                     e_s.at[c, h, d], e_r.at[c, h, d], ring_peer[h](by),
                 )
 
@@ -307,65 +308,68 @@
             own_e[c][h].wait()
             for d in range(3):
                 moved[c][h][d].wait_recv()
-            vecs = split(ebuf[h, c].reshape(SIDE * ROWS, PART))
+            vecs = split(ebuf[h, :, rows(c), :].reshape(SIDE * SIZES[c], PART))
             terms.append(products_of((vhigh[h], vlow[h]), vecs))
-        psend[:, c] = jnp.concatenate(terms, axis=1).T.reshape(2, SIDE, ROWS, 512)
+        psend[:, :, rows(c), :] = jnp.concatenate(terms, axis=1).T.reshape(2, SIDE, SIZES[c], 512)
         for h in both:
             for d, by in enumerate(OFFSETS):
                 w[c][h][d] = send(
-                    psend.at[h, c, shift(ring[h], by)],
-                    precv.at[c, h, d], w_s.at[c, h, d], w_r.at[c, h, d], ring_peer[h](by),
+                    psend.at[h, shift(ring[h], by), rows(c)],
+                    precv.at[h, d, rows(c)], w_s.at[c, h, d], w_r.at[c, h, d], ring_peer[h](by),
                 )
 
     def plane_sum(c):
-        total = psend[0, c, x] + psend[1, c, y]
+        total = psend[0, x, rows(c), :] + psend[1, y, rows(c), :]
         for h in both:
             for d in range(3):
                 w[c][h][d].wait_recv()
-                total = total + precv[c, h, d]
-        zsend[c] = total
+                total = total + precv[h, d, rows(c), :]
+        zsend[rows(c), :] = total
         zs[c] = [
-            send(zsend.at[c], zrecv.at[c, d], z_s.at[c, d], z_r.at[c, d], along_z(by)) for d, by in enumerate(OFFSETS)
+            send(zsend.at[rows(c)], zrecv.at[d, rows(c)], z_s.at[c, d], z_r.at[c, d], along_z(by)) for d, by in enumerate(OFFSETS)
         ]
 
     def coefficients(c):
-        total = zsend[c]
+        total = zsend[rows(c), :]
         for copy in own_t if c == 0 else []:
             copy.wait()
         for d in range(3):
             zs[c][d].wait_recv()
-            total = total + zrecv[c, d]
+            total = total + zrecv[d, rows(c), :]
         first, second = total[:, :256], total[:, 256:]
         coef_second = inner_full(second, t2[...])
         coef_first = inner_full(first, t1[...])
         for h in both:
-            xbuf[h, c, ring[h], :, pl.ds(0, 256)] = coef_first
-            xbuf[h, c, ring[h], :, pl.ds(256, 256)] = coef_second
-        for h in both:
-            mine = xbuf.at[h, c, ring[h]]
+            xbuf[h, ring[h], rows(c), pl.ds(0, 256)] = coef_first
+            xbuf[h, ring[h], rows(c), pl.ds(256, 256)] = coef_second
+        for h in both:
+            mine = xbuf.at[h, ring[h], rows(c)]
             for d, by in enumerate(OFFSETS):
                 xs[c][h][d] = send(mine, mine, x_s.at[c, h, d], x_r.at[c, h, d], ring_peer[h](by))
 
     def update(c):
+        count = SIDE * SIZES[c]
         for h in both:
             for d in range(3):
                 xs[c][h][d].wait_recv()
-            first, second = (xbuf[h, c, :, :, pl.ds(p * 256, 256)].reshape(SIDE * ROWS, 256) for p in both)
-            first = first - inner_full(second, t1_gram[...])
-            coefs = split(jnp.concatenate([first, second], axis=1))
-            for tile in range(TILES):
-                cols = pl.ds(tile * TILE, TILE)
+        first, second = (xbuf[:, :, rows(c), pl.ds(p * 256, 256)].reshape(2 * count, 256) for p in both)
+        first = first - inner_full(second, t1_gram[...])
+        high, low = split(jnp.concatenate([first, second], axis=1))
+        for tile in range(TILES):
+            cols = pl.ds(tile * TILE, TILE)
+            for h in both:
+                coefs = (high[h * count : (h + 1) * count], low[h * count : (h + 1) * count])
                 change = combine(coefs, (vhigh[h, :, cols], vlow[h, :, cols]))
-                obuf[h, c, :, :, cols] = ebuf[h, c, :, :, cols] - change.reshape(SIDE, ROWS, TILE)
+                obuf[h, :, rows(c), cols] = ebuf[h, :, rows(c), cols] - change.reshape(SIDE, SIZES[c], TILE)
                 there = pl.ds(pl.multiple_of(h * HALF + ring[h] * PART + tile * TILE, TILE), TILE)
                 for d, by in enumerate(OFFSETS):
                     back.append(
                         send(
-                            obuf.at[h, c, shift(ring[h], by), :, cols], out_ref.at[rows(c), there],
+                            obuf.at[h, shift(ring[h], by), rows(c), cols], out_ref.at[rows(c), there],
                             o_s.at[c, h, tile, d], o_r.at[c, h, tile, d], ring_peer[h](by),
                         )
                     )
-                stays.append(bring(obuf.at[h, c, ring[h], :, cols], out_ref.at[rows(c), there], own_sem.at[c, h, tile]))
+                stays.append(bring(obuf.at[h, ring[h], rows(c), cols], out_ref.at[rows(c), there], own_sem.at[c, h, tile]))
 
     stays = []
     move(1)
@@ -419,16 +423,16 @@
             vmem((2, 2, 4, 4, 2, 8, PART), F32),
             vmem((2, 512, PART), BF16),
             vmem((2, 512, PART), BF16),
-            vmem((2, CHUNKS, SIDE, ROWS, PART), F32),
-            vmem((2, CHUNKS, SIDE, ROWS, PART), F32),
+            vmem((2, SIDE, MINE, PART), F32),
+            vmem((2, SIDE, MINE, PART), F32),
             vmem((256, 256), F32),
             vmem((256, 256), F32),
             vmem((256, 256), F32),
-            vmem((2, CHUNKS, SIDE, ROWS, 512), F32),
-            vmem((CHUNKS, 2, 3, ROWS, 512), F32),
-            vmem((CHUNKS, ROWS, 512), F32),
-            vmem((CHUNKS, 3, ROWS, 512), F32),
-            vmem((2, CHUNKS, SIDE, ROWS, 512), F32),
+            vmem((2, SIDE, MINE, 512), F32),
+            vmem((2, 3, MINE, 512), F32),
+            vmem((MINE, 512), F32),
+            vmem((3, MINE, 512), F32),
+            vmem((2, SIDE, MINE, 512), F32),
             vmem((2, SIDE, 8, 256), F32),
             vmem((2, 3, 8, 256), F32),
             vmem((4, 4, 8, 256), F32),

time: 79 us -> 78.4 us (level)
  no operation moved by 1% of the time
where the time goes in v4:
time: 78.4 us; the launch traced here: 78.3 us
  Pallas kernels  78.3 us (100%)
    pallas_call x1, Pallas kernels, shards(): pl.pallas_call(body, out_shape=jax.ShapeDtypeStruct(evecs.shape, evecs.dt...  75.9 us
    pallas_call x1, Pallas kernels, shards(): pl.pallas_call(hand_over, out_shape=jax.ShapeDtypeStruct(evecs.shape, eve...  2.4 us

profile of v4, /device:TPU:0, one launch (start us, length us, event | category | flops | bytes accessed | tf_op | source)
XLA Modules:
  0.0 78.3 jit_solution(1465392898863220567)
XLA Ops:
  0.0 75.9 %back_transform.1.src = f32[32,16384]{1,0:T(8,128)} custom-call(f32[32,16384]{1,0:T(8,128)} %e_ref.1, f32[8,16384]{1,0:T(8,128)} %v1_ref.1, f32[8,16384]{1,0:T(8,128)} %v2_ref.1, f32[256,256]{1,0:T(8,128)} %t1_ref.1, f32[256,256]{1,0:T(8,128)} %t2_ref.1), custom_call_target="tpu_custom_call" | custom-call | tf_op jit(solution)/shard_map/back_transform/pallas_call | solution.py:417
  75.9 2.4 %hand_over.1 = f32[32,16384]{1,0:T(8,128)} custom-call(f32[32,16384]{1,0:T(8,128)} %back_transform.1.src), custom_call_target="tpu_custom_call" | custom-call | tf_op jit(solution)/shard_map/hand_over/pallas_call | solution.py:460

commit v5 on v4

--- a/solution.py
+++ b/solution.py
@@ -379,8 +379,8 @@
     step = gram_spread(step)
     products(1)
     step = gram_sum(step)
+    plane_sum(1)
     coefficients(0)
-    plane_sum(1)
     step = gram_partner(step)
     gram_use(step)
     coefficients(1)

time: 78.4 us -> 78.1 us (level)
  no operation moved by 1% of the time
where the time goes in v5:
time: 78.1 us; the launch traced here: 78 us
  Pallas kernels  77.9 us (100%)
    pallas_call x1, Pallas kernels, shards(): pl.pallas_call(body, out_shape=jax.ShapeDtypeStruct(evecs.shape, evecs.dt...  75.5 us
    pallas_call x1, Pallas kernels, shards(): pl.pallas_call(hand_over, out_shape=jax.ShapeDtypeStruct(evecs.shape, eve...  2.4 us

profile of v5, /device:TPU:0, one launch (start us, length us, event | category | flops | bytes accessed | tf_op | source)
XLA Modules:
  0.0 78.0 jit_solution(2271586989206740990)
XLA Ops:
  0.0 75.5 %back_transform.1.src = f32[32,16384]{1,0:T(8,128)} custom-call(f32[32,16384]{1,0:T(8,128)} %e_ref.1, f32[8,16384]{1,0:T(8,128)} %v1_ref.1, f32[8,16384]{1,0:T(8,128)} %v2_ref.1, f32[256,256]{1,0:T(8,128)} %t1_ref.1, f32[256,256]{1,0:T(8,128)} %t2_ref.1), custom_call_target="tpu_custom_call" | custom-call | tf_op jit(solution)/shard_map/back_transform/pallas_call | solution.py:417
  75.6 2.4 %hand_over.1 = f32[32,16384]{1,0:T(8,128)} custom-call(f32[32,16384]{1,0:T(8,128)} %back_transform.1.src), custom_call_target="tpu_custom_call" | custom-call | tf_op jit(solution)/shard_map/hand_over/pallas_call | solution.py:460

commit v6 on v5

--- a/solution.py
+++ b/solution.py
@@ -25,12 +25,6 @@
 
 def inner(left, right):
     return lax.dot_general(left, right, (((1,), (1,)), ((), ())), preferred_element_type=F32)
-
-
-def inner_full(left, right):
-    return lax.dot_general(
-        left, right, (((1,), (1,)), ((), ())), precision=HIGHEST, preferred_element_type=F32
-    )
 
 
 def plain(left, right):
@@ -295,7 +289,7 @@
     def gram_use(copies):
         for copy in copies:
             copy.wait_recv()
-        t1_gram[...] = plain_full(t1[...], gfull[...].reshape(256, 256))
+        t1_gram[...] = plain_full(t1[...].T, gfull[...].reshape(256, 256)).T
 
     w = [[[None] * 3 for _ in both] for _ in range(CHUNKS)]
     zs = [None] * CHUNKS
@@ -331,14 +325,12 @@
 
     def coefficients(c):
         total = zsend[rows(c), :]
-        for copy in own_t if c == 0 else []:
-            copy.wait()
         for d in range(3):
             zs[c][d].wait_recv()
             total = total + zrecv[d, rows(c), :]
         first, second = total[:, :256], total[:, 256:]
-        coef_second = inner_full(second, t2[...])
-        coef_first = inner_full(first, t1[...])
+        coef_second = plain_full(second, t2[...])
+        coef_first = plain_full(first, t1[...])
         for h in both:
             xbuf[h, ring[h], rows(c), pl.ds(0, 256)] = coef_first
             xbuf[h, ring[h], rows(c), pl.ds(256, 256)] = coef_second
@@ -353,7 +345,7 @@
             for d in range(3):
                 xs[c][h][d].wait_recv()
         first, second = (xbuf[:, :, rows(c), pl.ds(p * 256, 256)].reshape(2 * count, 256) for p in both)
-        first = first - inner_full(second, t1_gram[...])
+        first = first - plain_full(second, t1_gram[...])
         high, low = split(jnp.concatenate([first, second], axis=1))
         for tile in range(TILES):
             cols = pl.ds(tile * TILE, TILE)
@@ -373,6 +365,9 @@
 
     stays = []
     move(1)
+    for copy, factor in zip(own_t, (t1, t2)):
+        copy.wait()
+        factor[...] = factor[...].T
     products(0)
     step = gram_rows()
     plane_sum(0)

time: 78.1 us -> 78.2 us (level)
  no operation moved by 1% of the time
where the time goes in v6:
time: 78.2 us; the launch traced here: 78 us
  Pallas kernels  78 us (100%)
    pallas_call x1, Pallas kernels, shards(): pl.pallas_call(body, out_shape=jax.ShapeDtypeStruct(evecs.shape, evecs.dt...  75.6 us
    pallas_call x1, Pallas kernels, shards(): pl.pallas_call(hand_over, out_shape=jax.ShapeDtypeStruct(evecs.shape, eve...  2.4 us

profile of v6, /device:TPU:0, one launch (start us, length us, event | category | flops | bytes accessed | tf_op | source)
XLA Modules:
  0.0 78.0 jit_solution(15015493694564087211)
XLA Ops:
  0.0 75.6 %back_transform.1.src = f32[32,16384]{1,0:T(8,128)} custom-call(f32[32,16384]{1,0:T(8,128)} %e_ref.1, f32[8,16384]{1,0:T(8,128)} %v1_ref.1, f32[8,16384]{1,0:T(8,128)} %v2_ref.1, f32[256,256]{1,0:T(8,128)} %t1_ref.1, f32[256,256]{1,0:T(8,128)} %t2_ref.1), custom_call_target="tpu_custom_call" | custom-call | tf_op jit(solution)/shard_map/back_transform/pallas_call | solution.py:412
  75.6 2.4 %hand_over.1 = f32[32,16384]{1,0:T(8,128)} custom-call(f32[32,16384]{1,0:T(8,128)} %back_transform.1.src), custom_call_target="tpu_custom_call" | custom-call | tf_op jit(solution)/shard_map/hand_over/pallas_call | solution.py:455
